TPU v7x, 512 devices: a whole 4x4x16 slice. The times are simulated.
512 devices in a mesh: slab: 32 (over y, x, core), tile: 16 (over z).
Axes of the slice: x: 4, y: 4, z: 16, core: 2. Of those that a mesh axis runs over, the one named last changes fastest.
Arguments:
- history: bfloat16 [32, 2048, 8, 128], P('slab', 'tile'), may hold values from -15 to 15
- positions: bfloat16 [32, 2048, 3, 128], P('slab', 'tile'), may hold values from 0 to 1
- kappa_old: float32 [32, 2048, 128], P('slab', 'tile'), may hold values from 0.2 to 2
- threshold: float32 [32, 2048, 128], P('slab', 'tile'), may hold values from 0.3 to 1.5
- pair_ids: int32 [32, 2048, 8], P('slab', 'tile'), may hold values from 0 to 2047, as said below
- reader_counts: int32 [32, 2048], P('slab', 'tile'), may hold values from 1 to 8, as said below
- brick_map: int32 [32, 2048], P('slab', 'tile'), may hold values from 0 to 511, as said below
- strain_disp: bfloat16 [1024, 128], replicated, may hold values from -0.1875 to 0.1875
- couple: float32 [128, 128], replicated, may hold values from -0.5 to 0.5
Outputs:
- damage: float32 [32, 2048, 128], P('slab', 'tile')
- residual: float32 [1024, 16, 128], P('slab', 'tile')
Inputs may be any that keep to these rules, and one draw needn't show every extreme that they name: pair_ids[s, r, 0] = r; the other sources may be any clusters of the same depth layer. Only the first reader_counts[s, r] entries of pair_ids[s, r] are used. `brick_map`: a cluster among clusters t * 128 to (t + 1) * 128 - 1 lies in a brick among bricks (t - 1) * 32 to (t + 2) * 32 - 1.
All inputs are finite; a program needn't handle non-finite values.
Results may differ from a plain program's by a relative error of at most 0.0054.
Values may be sent and summed in bfloat16 or wider, within the bound.
No kernel may reach another device: no remote copies, remote signals or barrier semaphores. Data moves between devices by JAX's collectives and lax.ppermute only.
A program may use at most 64 MiB of HBM per device.

v0:
```python
import jax
import jax.numpy as jnp
from jax import lax
from jax.sharding import PartitionSpec as P

PAIRS = 8
BR_DEV = 32
SHARP = 12.0
SOFTEN = 2.0


def passed_along(block, axis, distance):
    devices = range(lax.axis_size(axis))
    route = [(i - distance, i) for i in devices if i - distance in devices]
    return lax.ppermute(block, axis, route)


def padded_2(array, sides, width):
    for axis, dim in sides:
        peers, length = (lax.axis_size(axis), array.shape[dim])
        up = [(i, (i + 1) % peers) for i in range(peers - 1)]
        down = [(j, i) for i, j in up]
        last = lax.slice_in_dim(array, length - width, length, axis=dim)
        leading = lax.slice_in_dim(array, 0, width, axis=dim)
        before = lax.ppermute(last, axis, up)
        after = lax.ppermute(leading, axis, down)
        array = jnp.concatenate([before, array, after], axis=dim)
    return array


def local(
    history,
    positions,
    kappa_old,
    threshold,
    pair_ids,
    reader_counts,
    brick_map,
    strain_disp,
    couple,
):
    hist = history[0]
    clusters = hist.shape[0]
    columns = hist.shape[1]
    points = hist.shape[2]
    packed = jnp.concatenate([hist, positions[0]], axis=1)
    tile_at = lax.axis_index("tile")
    ids = pair_ids[0]
    source = lax.all_gather(packed, "tile", axis=0, tiled=True)
    blocks = jnp.take(source, ids, axis=0)
    here = positions[0].astype(jnp.float32)
    counts = reader_counts[0]
    numer = jnp.zeros((clusters, columns, points), jnp.float32)
    denom = jnp.zeros((clusters, points), jnp.float32)
    for entry in range(PAIRS):
        src_hist = blocks[:, entry, :columns, :]
        src_pos = blocks[:, entry, columns:, :].astype(jnp.float32)
        dist = jnp.zeros((clusters, points, points), jnp.float32)
        for axis_k in range(3):
            delta = here[:, axis_k, :, None] - src_pos[:, axis_k, None, :]
            dist = dist + delta * delta
        live = (entry < counts).astype(jnp.float32)[:, None, None]
        weight = (jnp.exp(-SHARP * dist) * live).astype(jnp.bfloat16)
        numer = numer + jnp.einsum(
            "rcj,rij->rci", src_hist, weight, preferred_element_type=jnp.float32
        )
        denom = denom + jnp.sum(weight.astype(jnp.float32), axis=2)
    averaged = numer / denom[:, None, :]
    kappa = jnp.maximum(jnp.maximum(kappa_old[0], averaged[:, 0, :]), threshold[0])
    damage_here = 1.0 - threshold[0] / kappa * jnp.exp(-(kappa - threshold[0]) / SOFTEN)
    effective = ((1.0 - damage_here)[:, None, :] * averaged).astype(jnp.bfloat16)
    term = jnp.dot(
        effective.reshape(clusters, columns * points),
        strain_disp,
        preferred_element_type=jnp.float32,
    )
    bricks = BR_DEV
    owner = brick_map[0]
    local_brick = owner - (tile_at - 1) * bricks
    rows_near = lax.iota(jnp.int32, 3 * bricks)
    onehot = (local_brick[None, :] == rows_near[:, None]).astype(jnp.float32)
    shares = jnp.dot(
        onehot, term, precision=lax.Precision.HIGHEST, preferred_element_type=jnp.float32
    )
    shares = shares.reshape(3, bricks, term.shape[1])
    from_lower = passed_along(shares[2], "tile", 1)
    from_upper = passed_along(shares[0], "tile", -1)
    force = shares[1] + from_lower + from_upper
    padded = padded_2(force, (("slab", 0),), 1)
    beside = padded[:-2] + padded[2:]
    residual_here = force + jnp.dot(
        beside, couple, precision=lax.Precision.HIGHEST, preferred_element_type=jnp.float32
    )
    return (damage_here[None, :, :], residual_here[:, None, :])


def solution(mesh):
    placed = (
        P("slab", "tile", None, None),
        P("slab", "tile", None, None),
        P("slab", "tile", None),
        P("slab", "tile", None),
        P("slab", "tile", None),
        P("slab", "tile"),
        P("slab", "tile"),
        P(),
        P(),
    )
    return jax.shard_map(
        local,
        mesh=mesh,
        in_specs=placed,
        out_specs=(P("slab", "tile", None), P("slab", "tile", None)),
        check_vma=False,
    )
```

profile of v0, /device:TPU:7, one launch (start us, length us, event | category | flops | bytes accessed | tf_op | source)
XLA Modules:
  0.0 307.6 jit_solution(755815150721862255)
XLA Ops:
  7.2 0.0 copy-start
  7.2 0.0 all-gather.2.cloned.1.call-start
  7.2 1.0 copy.83
  8.2 1.7 pad_maximum_fusion
  9.9 0.0 all-gather.2.cloned.1.call-update
  9.9 0.7 compare_select_fusion
  10.6 0.1 copy.43
  10.7 0.1 reshape.192
  10.8 0.7 subtract_bitcast_fusion
  11.5 0.7 fusion.36
  12.1 0.7 compare_and_fusion
  12.8 0.9 bitcast_convert_fusion
  13.8 79.4 %all-gather.2.cloned.1.call-done = bf16[2048,11,128]{2,0,1:T(8,128)(2,1)} async-done(((bf16[128,11,128]{2,0,1:T(8,128)(2,1)}), bf16[2048,11,128]{2,0,1:T(8,128)(2,1)}) %all-gather.2.cloned.1.call-update) | async-done | bytes 5767184 | tf_op jit(solution)/shard_map/all_gather | solution.py:49
  93.2 9.0 %copy.44 = bf16[2048,11,128]{2,1,0:T(8,128)(2,1)} copy(bf16[2048,11,128]{2,0,1:T(8,128)(2,1)} %all-gather.2.cloned.1.call-done) | data formatting | bytes 11534336 | tf_op jit(solution)/shard_map/all_gather | solution.py:49
  102.2 11.9 %gather_fusion = bf16[1024,11,128]{2,1,0:T(8,128)(2,1)} fusion(bf16[2048,11,128]{2,1,0:T(8,128)(2,1)} %copy.44, s32[1024]{0:T(1024)S(1)} %broadcast_clamp_fusion), kind=kCustom, calls=%fused_computation | custom fusion | bytes 5771264 | tf_op jit(solution)/shard_map/jit(_take)/gather | solution.py:50
  114.1 3.6 %copy_select_fusion = bf16[128,8,11,128]{3,2,0,1:T(8,128)(2,1)S(1)} fusion(bf16[128,8,11,128]{3,2,1,0:T(8,128)(2,1)} %bitcast.146, pred[128,8]{0,1:T(8,128)(4,1)S(1)} %compare_and_fusion), kind=kLoop, calls=%fused_computation.17 | loop fusion | flops 1441792 | bytes 5768192 | tf_op jit(solution)/shard_map/jit(_take)/select_n | solution.py:50
  117.7 0.3 fusion.16
  118.1 0.3 fusion.53
  118.4 0.3 fusion.55
  118.6 0.3 fusion.57
  118.9 13.0 %fusion = f32[128,8,128]{2,1,0:T(8,128)S(1)} fusion(f32[128]{0:T(128)S(1)} %get-tuple-element.61, f32[128,128]{1,0:T(8,128)S(1)} %bitcast.164, f32[128,128]{1,0:T(8,128)S(1)} %get-tuple-element.55, f32[128,128]{1,0:T(8,128)S(1)} %bitcast.166, f32[128,128]{1,0:T(8,128)S(1)} %get-tuple-element.56, f32[128,128]{1,0:T(8,128)S(1)} %bitcast.162, ...), kind=kOutput, calls=%fused_computation.18 | convolution fusion | flops 56623104 | bytes 1180160 | tf_op jit(solution)/shard_map/rcj,rij->rci/dot_general | solution.py:64
  131.9 13.0 %fusion.2 = f32[128,8,128]{2,1,0:T(8,128)S(1)} fusion(f32[128]{0:T(128)S(1)} %get-tuple-element.65, f32[128,128]{1,0:T(8,128)S(1)} %bitcast.176, f32[128,128]{1,0:T(8,128)S(1)} %bitcast.178, f32[128,128]{1,0:T(8,128)S(1)} %bitcast.174, f32[128,128]{1,0:T(8,128)S(1)} %get-tuple-element.55, f32[128,128]{1,0:T(8,128)S(1)} %get-tuple-element.56, ...), kind=kOutput, calls=%fused_computation.20 | convolution fusion | flops 56623104 | bytes 1180160 | tf_op jit(solution)/shard_map/rcj,rij->rci/dot_general | solution.py:64
  144.9 13.0 %fusion.3 = f32[128,8,128]{2,1,0:T(8,128)S(1)} fusion(f32[128]{0:T(128)S(1)} %get-tuple-element.64, f32[128,128]{1,0:T(8,128)S(1)} %bitcast.182, f32[128,128]{1,0:T(8,128)S(1)} %bitcast.180, f32[128,128]{1,0:T(8,128)S(1)} %bitcast.184, f32[128,128]{1,0:T(8,128)S(1)} %get-tuple-element.55, f32[128,128]{1,0:T(8,128)S(1)} %get-tuple-element.56, ...), kind=kOutput, calls=%fused_computation.21 | convolution fusion | flops 56623104 | bytes 1180160 | tf_op jit(solution)/shard_map/rcj,rij->rci/dot_general | solution.py:64
  157.9 25.4 %convert_reduce_fusion.7 = (f32[128,128]{1,0:T(8,128)S(1)}, f32[128,128]{1,0:T(8,128)S(1)}, f32[128,128]{1,0:T(8,128)S(1)}, f32[128,128]{1,0:T(8,128)S(1)}) fusion(f32[128]{0:T(128)S(1)} %get-tuple-element.61, f32[128,128]{1,0:T(8,128)S(1)} %bitcast.165, f32[128,128]{1,0:T(8,128)S(1)} %get-tuple-element.55, f32[128,128]{1,0:T(8,128)S(1)} %bitcast.167, ...), kind=kLoop, calls=%fused_computation.8 | loop fusion | flops 108986368 | bytes 1247232 | tf_op jit(solution)/shard_map/reduce_sum | solution.py:67
  183.3 13.0 %fusion.4 = f32[128,8,128]{2,1,0:T(8,128)S(1)} fusion(f32[128]{0:T(128)S(1)} %get-tuple-element.63, f32[128,128]{1,0:T(8,128)S(1)} %bitcast.189, f32[128,128]{1,0:T(8,128)S(1)} %bitcast.191, f32[128,128]{1,0:T(8,128)S(1)} %bitcast.187, f32[128,128]{1,0:T(8,128)S(1)} %get-tuple-element.55, f32[128,128]{1,0:T(8,128)S(1)} %get-tuple-element.56, ...), kind=kOutput, calls=%fused_computation.22 | convolution fusion | flops 56623104 | bytes 1180160 | tf_op jit(solution)/shard_map/rcj,rij->rci/dot_general | solution.py:64
  196.3 0.3 fusion.59
  196.6 13.0 %fusion.1 = f32[128,8,128]{2,1,0:T(8,128)S(1)} fusion(f32[128]{0:T(128)S(1)} %get-tuple-element.66, f32[128,128]{1,0:T(8,128)S(1)} %bitcast.152, f32[128,128]{1,0:T(8,128)S(1)} %bitcast.150, f32[128,128]{1,0:T(8,128)S(1)} %bitcast.154, f32[128,128]{1,0:T(8,128)S(1)} %get-tuple-element.55, f32[128,128]{1,0:T(8,128)S(1)} %get-tuple-element.56, ...), kind=kOutput, calls=%fused_computation.19 | convolution fusion | flops 56623104 | bytes 1180160 | tf_op jit(solution)/shard_map/rcj,rij->rci/dot_general | solution.py:64
  209.5 13.0 %fusion.5 = f32[128,8,128]{2,1,0:T(8,128)S(1)} fusion(f32[128]{0:T(128)S(1)} %get-tuple-element.62, f32[128,128]{1,0:T(8,128)S(1)} %bitcast.158, f32[128,128]{1,0:T(8,128)S(1)} %bitcast.156, f32[128,128]{1,0:T(8,128)S(1)} %bitcast.160, f32[128,128]{1,0:T(8,128)S(1)} %get-tuple-element.55, f32[128,128]{1,0:T(8,128)S(1)} %get-tuple-element.56, ...), kind=kOutput, calls=%fused_computation.23 | convolution fusion | flops 56623104 | bytes 1180160 | tf_op jit(solution)/shard_map/rcj,rij->rci/dot_general | solution.py:64
  222.5 13.0 %fusion.6 = f32[128,8,128]{2,1,0:T(8,128)S(1)} fusion(f32[128]{0:T(128)S(1)} %get-tuple-element.68, f32[128,128]{1,0:T(8,128)S(1)} %bitcast.194, f32[128,128]{1,0:T(8,128)S(1)} %bitcast.196, f32[128,128]{1,0:T(8,128)S(1)} %bitcast.192, f32[128,128]{1,0:T(8,128)S(1)} %get-tuple-element.55, f32[128,128]{1,0:T(8,128)S(1)} %get-tuple-element.56, ...), kind=kOutput, calls=%fused_computation.24 | convolution fusion | flops 56623104 | bytes 1180160 | tf_op jit(solution)/shard_map/rcj,rij->rci/dot_general | solution.py:64
  235.5 25.4 %convert_reduce_fusion.6 = (f32[128,128]{1,0:T(8,128)S(1)}, f32[128,128]{1,0:T(8,128)S(1)}, f32[128,128]{1,0:T(8,128)S(1)}, f32[128,128]{1,0:T(8,128)S(1)}) fusion(f32[128]{0:T(128)S(1)} %get-tuple-element.66, f32[128,128]{1,0:T(8,128)S(1)} %bitcast.153, f32[128,128]{1,0:T(8,128)S(1)} %get-tuple-element.55, f32[128,128]{1,0:T(8,128)S(1)} %bitcast.151, ...), kind=kLoop, calls=%fused_computation.7 | loop fusion | flops 108986368 | bytes 1247232 | tf_op jit(solution)/shard_map/reduce_sum | solution.py:67
  260.9 0.0 copy-start.1
  260.9 0.0 copy-start.2
  260.9 0.0 copy-start.3
  261.0 13.0 %fusion.7 = f32[128,8,128]{2,1,0:T(8,128)S(1)} fusion(f32[128]{0:T(128)S(1)} %get-tuple-element.67, f32[128,128]{1,0:T(8,128)S(1)} %bitcast.171, f32[128,128]{1,0:T(8,128)S(1)} %bitcast.169, f32[128,128]{1,0:T(8,128)S(1)} %bitcast.173, f32[128,128]{1,0:T(8,128)S(1)} %get-tuple-element.55, f32[128,128]{1,0:T(8,128)S(1)} %get-tuple-element.56, ...), kind=kOutput, calls=%fused_computation.25 | convolution fusion | flops 56623104 | bytes 1180160 | tf_op jit(solution)/shard_map/rcj,rij->rci/dot_general | solution.py:64
  274.0 0.6 fusion.8
  274.7 0.2 copy.55
  274.9 0.3 fusion.63
  275.2 0.2 fusion.29
  275.4 3.0 collective-permute-start
  278.3 1.3 collective-permute-start.1
  279.6 0.0 collective-permute-done
  279.6 3.2 %collective-permute-done.1 = f32[32,128]{1,0:T(8,128)S(1)} collective-permute-done((f32[32,128]{1,0:T(8,128)S(1)}, f32[32,128]{1,0:T(8,128)S(1)}, u32[]{:S(2)}, u32[]{:S(2)}) %collective-permute-start.1) | collective-permute-done | bytes 16416 | tf_op jit(solution)/shard_map/ppermute | solution.py:15
  282.8 10.2 %collective-permute-start.2 = (f32[1,128]{1,0:T(1,128)S(1)}, f32[1,128]{1,0:T(1,128)S(1)}, u32[]{:S(2)}, u32[]{:S(2)}) collective-permute-start(f32[1,128]{1,0:T(1,128)S(1)} %get-tuple-element.59), channel_id=1, source_target_pairs={{0,16},{16,32},{32,48},{48,64},{64,80},{80,96},{96,112},{112,128},... | collective-permute-start | bytes 1544 | tf_op jit(solution)/shard_map/ppermute | solution.py:25
  293.0 1.9 collective-permute-start.3
  294.9 0.7 fusion.18
  295.6 0.0 collective-permute-done.2
  295.6 4.4 %collective-permute-done.3 = f32[1,128]{1,0:T(1,128)S(1)} collective-permute-done((f32[1,128]{1,0:T(1,128)S(1)}, f32[1,128]{1,0:T(1,128)S(1)}, u32[]{:S(2)}, u32[]{:S(2)}) %collective-permute-start.3) | collective-permute-done | bytes 544 | tf_op jit(solution)/shard_map/ppermute | solution.py:26
  300.0 0.8 convolution_add_fusion
  (12 shorter events, 0.2 us)
Async XLA Ops:
  7.2 267.7 %copy-start = (bf16[1024,128]{1,0:T(8,128)(2,1)S(1)}, bf16[1024,128]{1,0:T(8,128)(2,1)}, u32[]{:S(2)}) copy-start(bf16[1024,128]{1,0:T(8,128)(2,1)} %param.16) | copy-start | bytes 786436
  7.2 86.0 %all-gather.2.cloned.1.call-start = ((), (), s32[]{:S(2)}) async-start(), calls=%async_computation | async-start | bytes 6127616 | tf_op jit(solution)/shard_map/all_gather | solution.py:49
  260.9 13.7 %copy-start.1 = (f32[1,128,128]{2,1,0:T(8,128)S(1)}, f32[1,128,128]{2,1,0:T(8,128)}, u32[]{:S(2)}) copy-start(f32[1,128,128]{2,1,0:T(8,128)} %param.12) | copy-start | bytes 196612
  260.9 13.7 %copy-start.2 = (f32[1,128,128]{2,1,0:T(8,128)S(1)}, f32[1,128,128]{2,1,0:T(8,128)}, u32[]{:S(2)}) copy-start(f32[1,128,128]{2,1,0:T(8,128)} %param.11) | copy-start | bytes 196612
  260.9 39.0 %copy-start.3 = (f32[128,128]{1,0:T(8,128)S(1)}, f32[128,128]{1,0:T(8,128)}, u32[]{:S(2)}) copy-start(f32[128,128]{1,0:T(8,128)} %param.17) | copy-start | bytes 196612
  275.4 4.3 %collective-permute-start = (f32[32,128]{1,0:T(8,128)S(1)}, f32[32,128]{1,0:T(8,128)S(1)}, u32[]{:S(2)}, u32[]{:S(2)}) collective-permute-start(f32[32,128]{1,0:T(8,128)S(1)} %get-tuple-element.57), channel_id=1, source_target_pairs={{0,1},{1,2},{2,3},{3,4},{4,5},{5,6},{6,7},{7,8},{8,9},{9,10},{10,1... | collective-permute-start | bytes 49160 | tf_op jit(solution)/shard_map/ppermute | solution.py:15
  278.3 4.5 %collective-permute-start.1 = (f32[32,128]{1,0:T(8,128)S(1)}, f32[32,128]{1,0:T(8,128)S(1)}, u32[]{:S(2)}, u32[]{:S(2)}) collective-permute-start(f32[32,128]{1,0:T(8,128)S(1)} %get-tuple-element.58), channel_id=1, source_target_pairs={{1,0},{2,1},{3,2},{4,3},{5,4},{6,5},{7,6},{8,7},{9,8},{10,9},{11,1... | collective-permute-start | bytes 49160 | tf_op jit(solution)/shard_map/ppermute | solution.py:15
  282.8 12.8 %collective-permute-start.2 = (f32[1,128]{1,0:T(1,128)S(1)}, f32[1,128]{1,0:T(1,128)S(1)}, u32[]{:S(2)}, u32[]{:S(2)}) collective-permute-start(f32[1,128]{1,0:T(1,128)S(1)} %get-tuple-element.59), channel_id=1, source_target_pairs={{0,16},{16,32},{32,48},{48,64},{64,80},{80,96},{96,112},{112,128},... | collective-permute-start | bytes 1544 | tf_op jit(solution)/shard_map/ppermute | solution.py:25
  293.0 7.0 %collective-permute-start.3 = (f32[1,128]{1,0:T(1,128)S(1)}, f32[1,128]{1,0:T(1,128)S(1)}, u32[]{:S(2)}, u32[]{:S(2)}) collective-permute-start(f32[1,128]{1,0:T(1,128)S(1)} %get-tuple-element.60), channel_id=1, source_target_pairs={{16,0},{32,16},{48,32},{64,48},{80,64},{96,80},{112,96},{128,112},... | collective-permute-start | bytes 1544 | tf_op jit(solution)/shard_map/ppermute | solution.py:26
Sparse Core Ops, SparseCore 0:
  10.1 83.0 all-gather.1
where the time goes:
time: 308 us
  matrix products  105 us (34%)
  waiting for transfers between devices  87 us (28%)
  other arithmetic  61.5 us (20%)
  local copies, waits for them, and re-layouts  23.4 us (8%)
  starting transfers between devices  16.4 us (5%)
  between operations  14.3 us (5%)
    dot_general x8, matrix products, local(): jnp.einsum('rcj,rij->rci', src_hist, weight, preferred_element_type=jnp.f...  104 us
    all_gather x1, waiting for transfers between devices, local(): source = lax.all_gather(packed, 'tile', axis=0, tiled=True)  79.4 us
    reduce_sum x2, other arithmetic, local(): denom = denom + jnp.sum(weight.astype(jnp.float32), axis=2)  50.8 us
    gather x1, local copies, waits for them, and re-layouts, local(): blocks = jnp.take(source, ids, axis=0)  11.9 us
    ppermute x1, starting transfers between devices, padded_2(): before = lax.ppermute(last, axis, up)  10.2 us
    all_gather x1, local copies, waits for them, and re-layouts, local(): source = lax.all_gather(packed, 'tile', axis=0, tiled=True)  9.01 us
  transfers between devices with their start and end apart: 5, of which 3 were waited for; matrix products, arithmetic and copies ran while one was open for 1% of the time, Pallas kernels for 0%

commit v1 on v0

--- a/solution.py
+++ b/solution.py
@@ -46,7 +46,8 @@
     packed = jnp.concatenate([hist, positions[0]], axis=1)
     tile_at = lax.axis_index("tile")
     ids = pair_ids[0]
-    source = lax.all_gather(packed, "tile", axis=0, tiled=True)
+    repeated = jnp.stack([packed] * lax.axis_size("tile"))
+    source = jnp.concatenate(lax.all_to_all(repeated, "tile", 0, 0), axis=0)
     blocks = jnp.take(source, ids, axis=0)
     here = positions[0].astype(jnp.float32)
     counts = reader_counts[0]

time: 308 us -> 478 us (1.55)
  waiting for transfers between devices: 87 us -> 256 us
  between operations: 14.3 us -> 1 us
  starting transfers between devices: 16.4 us -> 28.4 us
  local copies, waits for them, and re-layouts: 23.4 us -> 29.2 us
    all_to_all x0 -> x1, waiting for transfers between devices: none -> 249 us  [local(): source = jnp.concatenate(lax.all_to_all(repeated, 'tile', 0, 0), axis=0)]
    all_gather x1 -> x0, waiting for transfers between devices: 79.4 us -> none  [local(): source = lax.all_gather(packed, 'tile', axis=0, tiled=True)]
    all_to_all x0 -> x1, starting transfers between devices: none -> 15 us  [local(): source = jnp.concatenate(lax.all_to_all(repeated, 'tile', 0, 0), axis=0)]
    all_to_all x0 -> x1, local copies, waits for them, and re-layouts: none -> 10.8 us  [local(): source = jnp.concatenate(lax.all_to_all(repeated, 'tile', 0, 0), axis=0)]
    all_gather x1 -> x0, local copies, waits for them, and re-layouts: 9.01 us -> none  [local(): source = lax.all_gather(packed, 'tile', axis=0, tiled=True)]
  transfers between devices with their start and end apart: 5 -> 5, of which waited for: 3 -> 3; matrix products, arithmetic and copies ran while one was open for 1% -> 0% of each run, Pallas kernels for 0% -> 0%
where the time goes in v1:
time: 478 us; the launch traced here: 477 us
  waiting for transfers between devices  256 us (54%)
  matrix products  105 us (22%)
  other arithmetic  57.5 us (12%)
  local copies, waits for them, and re-layouts  29.2 us (6%)
  starting transfers between devices  28.4 us (6%)
    all_to_all x1, waiting for transfers between devices, local(): source = jnp.concatenate(lax.all_to_all(repeated, 'tile', 0, 0), axis=0)  249 us
    dot_general x8, matrix products, local(): jnp.einsum('rcj,rij->rci', src_hist, weight, preferred_element_type=jnp.f...  104 us
    reduce_sum x2, other arithmetic, local(): denom = denom + jnp.sum(weight.astype(jnp.float32), axis=2)  51 us
    all_to_all x1, starting transfers between devices, local(): source = jnp.concatenate(lax.all_to_all(repeated, 'tile', 0, 0), axis=0)  15 us
    gather x1, local copies, waits for them, and re-layouts, local(): blocks = jnp.take(source, ids, axis=0)  11.8 us
    all_to_all x1, local copies, waits for them, and re-layouts, local(): source = jnp.concatenate(lax.all_to_all(repeated, 'tile', 0, 0), axis=0)  10.8 us
  transfers between devices with their start and end apart: 5, of which 3 were waited for; matrix products, arithmetic and copies ran while one was open for 0% of the time, Pallas kernels for 0%

profile of v1, /device:TPU:7, one launch (start us, length us, event | category | flops | bytes accessed | tf_op | source)
XLA Modules:
  0.0 477.5 jit_solution(17441480228001423938)
XLA Ops:
  0.6 0.0 copy-start
  0.6 1.0 copy.44
  1.7 1.1 pad_maximum_fusion
  2.7 0.1 copy.45
  2.9 0.0 copy-start.5
  2.9 0.0 copy-start.7
  2.9 0.0 copy-start.6
  2.9 0.0 copy-start.1
  2.9 3.9 stack.2
  6.8 15.0 %all-to-all-start = ((bf16[16,128,11,128]{3,1,2,0:T(8,128)(2,1)}), bf16[16,128,11,128]{3,1,2,0:T(8,128)(2,1)}, u32[]{:S(2)}, u32[]{:S(2)}) async-start(bf16[16,128,11,128]{3,1,2,0:T(8,128)(2,1)} %stack.2), calls=%async_computation | async-start | bytes 11534336 | tf_op jit(solution)/shard_map/all_to_all | solution.py:50
  21.8 0.1 copy.47
  21.9 0.1 reshape.198
  22.2 248.9 %all-to-all-done = bf16[16,128,11,128]{3,1,2,0:T(8,128)(2,1)} async-done(((bf16[16,128,11,128]{3,1,2,0:T(8,128)(2,1)}), bf16[16,128,11,128]{3,1,2,0:T(8,128)(2,1)}, u32[]{:S(2)}, u32[]{:S(2)}) %all-to-all-start) | async-done | bytes 5767200 | tf_op jit(solution)/shard_map/all_to_all | solution.py:50
  271.0 10.8 %copy.46 = bf16[16,128,11,128]{3,2,1,0:T(8,128)(2,1)} copy(bf16[16,128,11,128]{3,1,2,0:T(8,128)(2,1)} %all-to-all-done) | data formatting | bytes 11534336 | tf_op jit(solution)/shard_map/all_to_all | solution.py:50
  281.8 11.8 %gather_fusion = bf16[1024,11,128]{2,1,0:T(8,128)(2,1)} fusion(bf16[2048,11,128]{2,1,0:T(8,128)(2,1)} %bitcast.145, s32[1024]{0:T(1024)S(1)} %broadcast_clamp_fusion), kind=kCustom, calls=%fused_computation | custom fusion | bytes 5771264 | tf_op jit(solution)/shard_map/jit(_take)/gather | solution.py:51
  293.6 3.6 copy_select_fusion
  297.2 0.3 fusion.16
  297.6 0.3 fusion.53
  297.8 0.3 fusion.55
  298.1 0.3 fusion.57
  298.4 13.0 %fusion = f32[128,8,128]{2,1,0:T(8,128)S(1)} fusion(f32[128]{0:T(128)S(1)} %get-tuple-element.61, f32[128,128]{1,0:T(8,128)S(1)} %bitcast.164, f32[128,128]{1,0:T(8,128)S(1)} %get-tuple-element.55, f32[128,128]{1,0:T(8,128)S(1)} %bitcast.166, f32[128,128]{1,0:T(8,128)S(1)} %get-tuple-element.56, f32[128,128]{1,0:T(8,128)S(1)} %bitcast.162, ...), kind=kOutput, calls=%fused_computation.18 | convolution fusion | flops 56623104 | bytes 1180160 | tf_op jit(solution)/shard_map/rcj,rij->rci/dot_general | solution.py:65
  311.4 13.0 %fusion.2 = f32[128,8,128]{2,1,0:T(8,128)S(1)} fusion(f32[128]{0:T(128)S(1)} %get-tuple-element.65, f32[128,128]{1,0:T(8,128)S(1)} %bitcast.176, f32[128,128]{1,0:T(8,128)S(1)} %bitcast.178, f32[128,128]{1,0:T(8,128)S(1)} %bitcast.174, f32[128,128]{1,0:T(8,128)S(1)} %get-tuple-element.55, f32[128,128]{1,0:T(8,128)S(1)} %get-tuple-element.56, ...), kind=kOutput, calls=%fused_computation.20 | convolution fusion | flops 56623104 | bytes 1180160 | tf_op jit(solution)/shard_map/rcj,rij->rci/dot_general | solution.py:65
  324.4 13.0 %fusion.3 = f32[128,8,128]{2,1,0:T(8,128)S(1)} fusion(f32[128]{0:T(128)S(1)} %get-tuple-element.64, f32[128,128]{1,0:T(8,128)S(1)} %bitcast.182, f32[128,128]{1,0:T(8,128)S(1)} %bitcast.180, f32[128,128]{1,0:T(8,128)S(1)} %bitcast.184, f32[128,128]{1,0:T(8,128)S(1)} %get-tuple-element.55, f32[128,128]{1,0:T(8,128)S(1)} %get-tuple-element.56, ...), kind=kOutput, calls=%fused_computation.21 | convolution fusion | flops 56623104 | bytes 1180160 | tf_op jit(solution)/shard_map/rcj,rij->rci/dot_general | solution.py:65
  337.3 25.4 %convert_reduce_fusion.7 = (f32[128,128]{1,0:T(8,128)S(1)}, f32[128,128]{1,0:T(8,128)S(1)}, f32[128,128]{1,0:T(8,128)S(1)}, f32[128,128]{1,0:T(8,128)S(1)}) fusion(f32[128]{0:T(128)S(1)} %get-tuple-element.61, f32[128,128]{1,0:T(8,128)S(1)} %bitcast.165, f32[128,128]{1,0:T(8,128)S(1)} %get-tuple-element.55, f32[128,128]{1,0:T(8,128)S(1)} %bitcast.167, ...), kind=kLoop, calls=%fused_computation.8 | loop fusion | flops 108986368 | bytes 1247232 | tf_op jit(solution)/shard_map/reduce_sum | solution.py:68
  362.8 13.0 %fusion.4 = f32[128,8,128]{2,1,0:T(8,128)S(1)} fusion(f32[128]{0:T(128)S(1)} %get-tuple-element.63, f32[128,128]{1,0:T(8,128)S(1)} %bitcast.189, f32[128,128]{1,0:T(8,128)S(1)} %bitcast.191, f32[128,128]{1,0:T(8,128)S(1)} %bitcast.187, f32[128,128]{1,0:T(8,128)S(1)} %get-tuple-element.55, f32[128,128]{1,0:T(8,128)S(1)} %get-tuple-element.56, ...), kind=kOutput, calls=%fused_computation.22 | convolution fusion | flops 56623104 | bytes 1180160 | tf_op jit(solution)/shard_map/rcj,rij->rci/dot_general | solution.py:65
  375.8 0.3 fusion.59
  376.0 13.0 %fusion.1 = f32[128,8,128]{2,1,0:T(8,128)S(1)} fusion(f32[128]{0:T(128)S(1)} %get-tuple-element.66, f32[128,128]{1,0:T(8,128)S(1)} %bitcast.152, f32[128,128]{1,0:T(8,128)S(1)} %bitcast.150, f32[128,128]{1,0:T(8,128)S(1)} %bitcast.154, f32[128,128]{1,0:T(8,128)S(1)} %get-tuple-element.55, f32[128,128]{1,0:T(8,128)S(1)} %get-tuple-element.56, ...), kind=kOutput, calls=%fused_computation.19 | convolution fusion | flops 56623104 | bytes 1180160 | tf_op jit(solution)/shard_map/rcj,rij->rci/dot_general | solution.py:65
  389.0 13.0 %fusion.5 = f32[128,8,128]{2,1,0:T(8,128)S(1)} fusion(f32[128]{0:T(128)S(1)} %get-tuple-element.62, f32[128,128]{1,0:T(8,128)S(1)} %bitcast.158, f32[128,128]{1,0:T(8,128)S(1)} %bitcast.156, f32[128,128]{1,0:T(8,128)S(1)} %bitcast.160, f32[128,128]{1,0:T(8,128)S(1)} %get-tuple-element.55, f32[128,128]{1,0:T(8,128)S(1)} %get-tuple-element.56, ...), kind=kOutput, calls=%fused_computation.23 | convolution fusion | flops 56623104 | bytes 1180160 | tf_op jit(solution)/shard_map/rcj,rij->rci/dot_general | solution.py:65
  402.0 13.0 %fusion.6 = f32[128,8,128]{2,1,0:T(8,128)S(1)} fusion(f32[128]{0:T(128)S(1)} %get-tuple-element.68, f32[128,128]{1,0:T(8,128)S(1)} %bitcast.194, f32[128,128]{1,0:T(8,128)S(1)} %bitcast.196, f32[128,128]{1,0:T(8,128)S(1)} %bitcast.192, f32[128,128]{1,0:T(8,128)S(1)} %get-tuple-element.55, f32[128,128]{1,0:T(8,128)S(1)} %get-tuple-element.56, ...), kind=kOutput, calls=%fused_computation.24 | convolution fusion | flops 56623104 | bytes 1180160 | tf_op jit(solution)/shard_map/rcj,rij->rci/dot_general | solution.py:65
  415.0 25.6 %convert_reduce_fusion.6 = (f32[128,128]{1,0:T(8,128)S(1)}, f32[128,128]{1,0:T(8,128)S(1)}, f32[128,128]{1,0:T(8,128)S(1)}, f32[128,128]{1,0:T(8,128)S(1)}) fusion(f32[128]{0:T(128)S(1)} %get-tuple-element.66, f32[128,128]{1,0:T(8,128)S(1)} %bitcast.153, f32[128,128]{1,0:T(8,128)S(1)} %get-tuple-element.55, f32[128,128]{1,0:T(8,128)S(1)} %bitcast.151, ...), kind=kLoop, calls=%fused_computation.7 | loop fusion | flops 108986368 | bytes 1247232 | tf_op jit(solution)/shard_map/reduce_sum | solution.py:68
  440.6 0.0 copy-start.2
  440.6 0.0 copy-start.3
  440.6 0.0 copy-start.4
  440.6 13.0 %fusion.7 = f32[128,8,128]{2,1,0:T(8,128)S(1)} fusion(f32[128]{0:T(128)S(1)} %get-tuple-element.67, f32[128,128]{1,0:T(8,128)S(1)} %bitcast.171, f32[128,128]{1,0:T(8,128)S(1)} %bitcast.169, f32[128,128]{1,0:T(8,128)S(1)} %bitcast.173, f32[128,128]{1,0:T(8,128)S(1)} %get-tuple-element.55, f32[128,128]{1,0:T(8,128)S(1)} %get-tuple-element.56, ...), kind=kOutput, calls=%fused_computation.25 | convolution fusion | flops 56623104 | bytes 1180160 | tf_op jit(solution)/shard_map/rcj,rij->rci/dot_general | solution.py:65
  453.6 0.6 fusion.8
  454.4 0.2 copy.58
  454.6 0.3 fusion.63
  454.8 0.2 fusion.29
  455.0 4.3 collective-permute-start
  459.3 1.3 collective-permute-start.1
  460.6 0.0 collective-permute-done
  460.6 3.2 collective-permute-done.1
  463.8 5.9 %collective-permute-start.2 = (f32[1,128]{1,0:T(1,128)S(1)}, f32[1,128]{1,0:T(1,128)S(1)}, u32[]{:S(2)}, u32[]{:S(2)}) collective-permute-start(f32[1,128]{1,0:T(1,128)S(1)} %get-tuple-element.59), channel_id=1, source_target_pairs={{0,16},{16,32},{32,48},{48,64},{64,80},{80,96},{96,112},{112,128},... | collective-permute-start | bytes 1544 | tf_op jit(solution)/shard_map/ppermute | solution.py:25
  469.7 1.9 collective-permute-start.3
  471.6 0.7 fusion.18
  472.3 0.0 collective-permute-done.2
  472.3 4.4 collective-permute-done.3
  476.7 0.8 convolution_add_fusion
  (21 shorter events, 0.2 us)
Async XLA Ops:
  0.6 453.9 %copy-start = (bf16[1024,128]{1,0:T(8,128)(2,1)S(1)}, bf16[1024,128]{1,0:T(8,128)(2,1)}, u32[]{:S(2)}) copy-start(bf16[1024,128]{1,0:T(8,128)(2,1)} %param.16) | copy-start | bytes 786436
  2.9 19.0 %copy-start.5 = (s32[1,128,8]{1,2,0:T(8,128)S(1)}, s32[1,128,8]{1,2,0:T(8,128)}, u32[]{:S(2)}) copy-start(s32[1,128,8]{1,2,0:T(8,128)} %param.13) | copy-start | bytes 12292
  2.9 19.2 %copy-start.7 = (s32[1,128]{1,0:T(1,128)S(1)}, s32[1,128]{1,0:T(1,128)}, u32[]{:S(2)}) copy-start(s32[1,128]{1,0:T(1,128)} %param.15) | copy-start | bytes 1540
  2.9 19.2 %copy-start.6 = (s32[1,128]{1,0:T(1,128)S(1)}, s32[1,128]{1,0:T(1,128)}, u32[]{:S(2)}) copy-start(s32[1,128]{1,0:T(1,128)} %param.14) | copy-start | bytes 1540
  2.9 19.2 %copy-start.1 = (bf16[1,128,3,128]{3,1,2,0:T(8,128)(2,1)S(1)}, bf16[1,128,3,128]{3,1,2,0:T(8,128)(2,1)}, u32[]{:S(2)}) copy-start(bf16[1,128,3,128]{3,1,2,0:T(8,128)(2,1)} %param.10) | copy-start | bytes 294916
  6.8 264.2 %all-to-all-start = ((bf16[16,128,11,128]{3,1,2,0:T(8,128)(2,1)}), bf16[16,128,11,128]{3,1,2,0:T(8,128)(2,1)}, u32[]{:S(2)}, u32[]{:S(2)}) async-start(bf16[16,128,11,128]{3,1,2,0:T(8,128)(2,1)} %stack.2), calls=%async_computation | async-start | bytes 11534336 | tf_op jit(solution)/shard_map/all_to_all | solution.py:50
  440.6 13.7 %copy-start.2 = (f32[1,128,128]{2,1,0:T(8,128)S(1)}, f32[1,128,128]{2,1,0:T(8,128)}, u32[]{:S(2)}) copy-start(f32[1,128,128]{2,1,0:T(8,128)} %param.12) | copy-start | bytes 196612
  440.6 13.7 %copy-start.3 = (f32[1,128,128]{2,1,0:T(8,128)S(1)}, f32[1,128,128]{2,1,0:T(8,128)}, u32[]{:S(2)}) copy-start(f32[1,128,128]{2,1,0:T(8,128)} %param.11) | copy-start | bytes 196612
  440.6 36.1 %copy-start.4 = (f32[128,128]{1,0:T(8,128)S(1)}, f32[128,128]{1,0:T(8,128)}, u32[]{:S(2)}) copy-start(f32[128,128]{1,0:T(8,128)} %param.17) | copy-start | bytes 196612
  455.0 5.6 %collective-permute-start = (f32[32,128]{1,0:T(8,128)S(1)}, f32[32,128]{1,0:T(8,128)S(1)}, u32[]{:S(2)}, u32[]{:S(2)}) collective-permute-start(f32[32,128]{1,0:T(8,128)S(1)} %get-tuple-element.57), channel_id=1, source_target_pairs={{0,1},{1,2},{2,3},{3,4},{4,5},{5,6},{6,7},{7,8},{8,9},{9,10},{10,1... | collective-permute-start | bytes 49160 | tf_op jit(solution)/shard_map/ppermute | solution.py:15
  459.3 4.5 collective-permute-start.1
  463.8 8.5 %collective-permute-start.2 = (f32[1,128]{1,0:T(1,128)S(1)}, f32[1,128]{1,0:T(1,128)S(1)}, u32[]{:S(2)}, u32[]{:S(2)}) collective-permute-start(f32[1,128]{1,0:T(1,128)S(1)} %get-tuple-element.59), channel_id=1, source_target_pairs={{0,16},{16,32},{32,48},{48,64},{64,80},{80,96},{96,112},{112,128},... | collective-permute-start | bytes 1544 | tf_op jit(solution)/shard_map/ppermute | solution.py:25
  469.7 7.0 %collective-permute-start.3 = (f32[1,128]{1,0:T(1,128)S(1)}, f32[1,128]{1,0:T(1,128)S(1)}, u32[]{:S(2)}, u32[]{:S(2)}) collective-permute-start(f32[1,128]{1,0:T(1,128)S(1)} %get-tuple-element.60), channel_id=1, source_target_pairs={{16,0},{32,16},{48,32},{64,48},{80,64},{96,80},{112,96},{128,112},... | collective-permute-start | bytes 1544 | tf_op jit(solution)/shard_map/ppermute | solution.py:26
